TPU v7x, 32 devices: a whole 2x2x4 slice. The times are simulated.
32 devices in a mesh: head: 2 (over y), seq: 4 (over z), dp: 4 (over x, core).
Axes of the slice: x: 2, y: 2, z: 4, core: 2. Of those that a mesh axis runs over, the one named last changes fastest.
Arguments:
- teacher_query: bfloat16 [4, 512, 3072], P('dp', 'seq', 'head'), may hold values from -6 to 6
- teacher_key: bfloat16 [4, 512, 3072], P('dp', 'seq', 'head'), may hold values from -6 to 6
- student_query: bfloat16 [4, 512, 512], P('dp', 'seq'), may hold values from -6 to 6
- student_key: bfloat16 [4, 512, 512], P('dp', 'seq'), may hold values from -6 to 6
- head_mix: float32 [24, 8], P('head'), may hold values from 0.02 to 0.25
Outputs:
- grad_query: float32 [4, 512, 512], P('dp', 'seq', 'head')
- grad_key: float32 [4, 512, 512], P('dp', 'seq', 'head')
- grad_mix: float32 [24, 8], P('head')
- head_loss: float32 [24], P('head')
All inputs are finite; a program needn't handle non-finite values.
Results may differ from a plain program's by a relative error of at most 0.0012.
Values may be sent and summed in bfloat16 or wider, within the bound.
No kernel may reach another device: no remote copies, remote signals or barrier semaphores. Data moves between devices by JAX's collectives and lax.ppermute only.
A program may use at most 64 MiB of HBM per device.

v0:
```python
import math

import jax
import jax.numpy as jnp
from jax import lax
from jax.sharding import PartitionSpec as P

HEADS_T = 24
HD_T = 128
HEADS_S = 8
HD_S = 64


def from_behind(block, axis, distance):
    devices = range(lax.axis_size(axis))
    route = [((i - distance) % len(devices), i) for i in devices]
    return lax.ppermute(block, axis, route)


def lift_heads(head_mix, student):
    lifted = head_mix[:, 0, None, None] * student[0][None]
    for index in range(1, HEADS_S):
        lifted = lifted + head_mix[:, index, None, None] * student[index][None]
    return lifted


def block_maps(query_t, query_s, key_t, key_s, head_mix):
    row_count = query_t.shape[0]
    key_count = key_t.shape[0]
    teacher_heads = head_mix.shape[0]
    teacher = jnp.einsum(
        "rhd,khd->hrk",
        query_t.reshape(row_count, teacher_heads, HD_T),
        key_t.reshape(key_count, teacher_heads, HD_T),
        preferred_element_type=jnp.float32,
    ) * HD_T ** (-0.5)
    student = jnp.einsum(
        "rhd,khd->hrk",
        query_s.reshape(row_count, HEADS_S, HD_S),
        key_s.reshape(key_count, HEADS_S, HD_S),
        preferred_element_type=jnp.float32,
    ) * HD_S ** (-0.5)
    lifted = lift_heads(head_mix, student)
    return (teacher, student, lifted)


def absorb(stats, teacher, lifted):
    top_t, total_t, top_l, total_l = stats
    new_t = jnp.maximum(top_t, jnp.max(teacher, axis=-1))
    new_l = jnp.maximum(top_l, jnp.max(lifted, axis=-1))
    total_t = total_t * jnp.exp(top_t - new_t) + jnp.sum(
        jnp.exp(teacher - new_t[..., None]), axis=-1
    )
    total_l = total_l * jnp.exp(top_l - new_l) + jnp.sum(
        jnp.exp(lifted - new_l[..., None]), axis=-1
    )
    return (new_t, total_t, new_l, total_l)


def pair_terms(query_t, query_s, key_t, key_s, head_mix, lse_t, lse_l):
    teacher, student, lifted = block_maps(query_t, query_s, key_t, key_s, head_mix)
    prob_t = jnp.exp(teacher - lse_t[..., None])
    prob_l = jnp.exp(lifted - lse_l[..., None])
    kl_part = jnp.sum(prob_t * (teacher - lifted), axis=-1)
    excess = prob_l - prob_t
    mix_columns = []
    mixed_rows = []
    for index in range(HEADS_S):
        mix_columns.append(jnp.sum(excess * student[index][None], axis=(1, 2)))
        mixed_rows.append(jnp.sum(head_mix[:, index, None, None] * excess, axis=0))
    mix_part = jnp.stack(mix_columns, axis=1)
    mixed_grad = jnp.stack(mixed_rows, axis=0).astype(jnp.bfloat16)
    return (kl_part, mix_part, mixed_grad)


def query_side(mixed_grad, key_s):
    key_count = key_s.shape[0]
    result = jnp.einsum(
        "hrk,khd->rhd",
        mixed_grad,
        key_s.reshape(key_count, HEADS_S, HD_S),
        preferred_element_type=jnp.float32,
    )
    return result.reshape(result.shape[0], HEADS_S * HD_S)


def key_side(mixed_grad, query_s):
    row_count = query_s.shape[0]
    result = jnp.einsum(
        "hrk,rhd->khd",
        mixed_grad,
        query_s.reshape(row_count, HEADS_S, HD_S),
        preferred_element_type=jnp.float32,
    )
    return result.reshape(result.shape[0], HEADS_S * HD_S)


def body(teacher_query, teacher_key, student_query, student_key, head_mix):
    query_t = teacher_query[0]
    query_s = student_query[0]
    own_t = teacher_key[0]
    own_s = student_key[0]
    row_count = query_t.shape[0]
    teacher_heads = head_mix.shape[0]
    group_size = lax.axis_size("seq")
    position = lax.axis_index("seq")
    shards_per = math.gcd(group_size, max(1, 512 // row_count))
    block_rows = shards_per * row_count
    block_count = group_size // shards_per
    gathered = (
        lax.all_gather(teacher_key, "seq", axis=1, tiled=True),
        lax.all_gather(student_key, "seq", axis=1, tiled=True),
    )
    keys_t = gathered[0][0]
    keys_s = gathered[1][0]

    def first_pass(index, stats):
        start = index * block_rows
        key_t = lax.dynamic_slice_in_dim(keys_t, start, block_rows, 0)
        key_s = lax.dynamic_slice_in_dim(keys_s, start, block_rows, 0)
        teacher, student, lifted = block_maps(query_t, query_s, key_t, key_s, head_mix)
        return absorb(stats, teacher, lifted)

    floor_value = jnp.full((teacher_heads, row_count), -1e30, jnp.float32)
    zero_rows = jnp.zeros((teacher_heads, row_count), jnp.float32)
    stats = lax.fori_loop(
        0, block_count, first_pass, (floor_value, zero_rows, floor_value, zero_rows)
    )
    lse_t = stats[0] + jnp.log(stats[1])
    lse_l = stats[2] + jnp.log(stats[3])
    kl_sum, mix_sum, mixed_grad = pair_terms(query_t, query_s, own_t, own_s, head_mix, lse_t, lse_l)
    query_grad = query_side(mixed_grad, own_s)
    carried = key_side(mixed_grad, query_s)

    def second_pass(turn, carry):
        kl_acc, mix_acc, query_acc, moving = carry
        moving = from_behind(moving, "seq", 1)
        start = (position - turn) % group_size * row_count
        key_t = lax.dynamic_slice_in_dim(keys_t, start, row_count, 0)
        key_s = lax.dynamic_slice_in_dim(keys_s, start, row_count, 0)
        kl_part, mix_part, mixed = pair_terms(
            query_t, query_s, key_t, key_s, head_mix, lse_t, lse_l
        )
        return (
            kl_acc + kl_part,
            mix_acc + mix_part,
            query_acc + query_side(mixed, key_s),
            moving + key_side(mixed, query_s),
        )

    kl_sum, mix_sum, query_grad, carried = lax.fori_loop(
        1, group_size, second_pass, (kl_sum, mix_sum, query_grad, carried)
    )
    key_grad = from_behind(carried, "seq", 1)
    seq_len = row_count * group_size
    images = lax.axis_size("dp") * teacher_query.shape[0]
    weight = seq_len / HEADS_T
    factor = weight * HD_S ** (-0.5)
    grad_query, grad_key = (
        lax.psum_scatter((query_grad * factor)[None], "head", scatter_dimension=2, tiled=True),
        lax.psum_scatter((key_grad * factor)[None], "head", scatter_dimension=2, tiled=True),
    )
    kl_rows = jnp.sum(kl_sum - lse_t + lse_l, axis=-1)
    mix_total, loss_total = lax.psum((mix_sum, kl_rows), ("seq", "dp"))
    grad_mix = mix_total * (weight / (images * seq_len))
    head_loss = loss_total / (images * seq_len)
    return (grad_query, grad_key, grad_mix, head_loss)


def solution(mesh):
    return jax.shard_map(
        body,
        mesh=mesh,
        in_specs=(
            P("dp", "seq", "head"),
            P("dp", "seq", "head"),
            P("dp", "seq", None),
            P("dp", "seq", None),
            P("head", None),
        ),
        out_specs=(P("dp", "seq", "head"), P("dp", "seq", "head"), P("head", None), P("head")),
        check_vma=False,
    )
```

profile of v0, /device:TPU:0, one launch (start us, length us, event | category | flops | bytes accessed | tf_op | source)
XLA Modules:
  0.0 139.3 jit_solution(742827363600972516)
XLA Ops:
  7.2 1.9 %copy.105 = bf16[1,128,1536]{1,2,0:T(8,128)(2,1)} copy(bf16[1,128,1536]{2,1,0:T(8,128)(2,1)} %param.8) | data formatting | bytes 786432 | tf_op args[1]
  9.2 1.0 copy.111
  10.2 1.0 copy.112
  11.3 1.2 copy.104
  13.6 23.6 %all_gather.7 = bf16[1,512,512]{1,2,0:T(8,128)(2,1)S(1)} all-gather(bf16[1,128,512]{1,2,0:T(8,128)(2,1)S(1)} %copy.112), channel_id=1, replica_groups=mesh['head'=2,'seq'=4,'dp'=4] {'seq'}, dimensions={1}, use_global_device_ids=true | all-gather | bytes 655360 | tf_op jit(solution)/shard_map/all_gather | solution.py:112
  37.9 2.1 %fusion.2 = f32[12,128]{1,0:T(8,128)S(1)} fusion(f32[128,512]{1,0:T(8,128)S(1)} %get-tuple-element.486, f32[12]{0:T(128)S(1)} %get-tuple-element.508, f32[128,512]{1,0:T(8,128)S(1)} %get-tuple-element.487, f32[12]{0:T(128)S(1)} %get-tuple-element.502, f32[128,512]{1,0:T(8,128)S(1)} %get-tuple-element.488, f32[12]{0:T(128)S(1)} %get-tuple-element.503, ...), kind=kLoop, calls=%fused_computation.56 | loop fusion | flops 12581376 | bytes 2103680 | tf_op jit(solution)/shard_map/while/body/eval_jaxpr/reduce_max | solution.py:50
  40.1 2.4 %exponential_reduce_fusion = f32[12,128]{1,0:T(8,128)S(1)} fusion(f32[12,128]{1,0:T(8,128)S(1)} %broadcast_maximum_fusion, f32[128,512]{1,0:T(8,128)S(1)} %get-tuple-element.486, f32[12]{0:T(128)S(1)} %get-tuple-element.508, f32[128,512]{1,0:T(8,128)S(1)} %get-tuple-element.487, f32[12]{0:T(128)S(1)} %get-tuple-element.502, ...), kind=kLoop, calls=%fused_computation.52 | loop fusion | flops 13367808 | bytes 2109824 | tf_op jit(solution)/shard_map/while/body/eval_jaxpr/reduce_sum | solution.py:54
  42.5 13.3 %all-gather.2.cloned.1.call-done = bf16[1,512,1536]{1,2,0:T(8,128)(2,1)} async-done(((bf16[1,128,1536]{1,2,0:T(8,128)(2,1)}), bf16[1,512,1536]{1,2,0:T(8,128)(2,1)}) %all-gather.2.cloned.1.call-update) | async-done | bytes 1572880 | tf_op jit(solution)/shard_map/all_gather | solution.py:111
  55.8 2.2 %multiply_reduce_fusion.17 = (f32[12,128]{1,0:T(8,128)S(1)}, f32[12,128,512]{2,1,0:T(8,128)S(1)}) fusion(bf16[128,12,128]{0,2,1:T(8,128)(2,1)S(1)} %bitcast.263, bf16[512,12,128]{0,2,1:T(8,128)(2,1)} %bitcast.257), kind=kOutput, calls=%fused_computation.55 | convolution fusion | flops 202897920 | bytes 5117952 | tf_op jit(solution)/shard_map/while/body/eval_jaxpr/rhd,khd->hrk/dot_general | solution.py:31
  58.0 1.0 exponential_reduce_fusion.1
  59.0 0.8 exponential_subtract_fusion.1
  59.8 2.3 %multiply_reduce_fusion.18 = (bf16[128,128]{0,1:T(8,128)(2,1)S(1)}, bf16[128,128]{0,1:T(8,128)(2,1)S(1)}, bf16[128,128]{0,1:T(8,128)(2,1)S(1)}, bf16[128,128]{0,...) fusion(f32[12,128,128]{1,2,0:T(8,128)S(1)} %get-tuple-element.5, ...), kind=kLoop, calls=%fused_computation.60 | loop fusion | flops 9894304 | bytes 2372352 | tf_op jit(solution)/shard_map/reduce_sum | solution.py:70
  63.7 27.8 %while.6 = (s32[]{:T(128)}, f32[12,128]{1,0:T(8,128)S(1)}, f32[12,8]{0,1:T(8,128)S(1)}, f32[128,512]{0,1:T(8,128)S(1)}, f32[128,512]{0,1:T(8,128)S(1)}, /*index=...) while((s32[]{:T(128)}, f32[12,128]{1,0:T(8,128)S(1)}, ...), condition=%wide.region_39.40_spmd, body=%wide.region_21.39_spmd.sunk | while | flops 114556944 | bytes 13154436 | solution.py:151
  64.2 1.0 constant_dynamic-slice_fusion.5
  66.0 2.2 %multiply_reduce_fusion.36 = (bf16[128,128]{0,1:T(8,128)(2,1)S(1)}, bf16[128,128]{0,1:T(8,128)(2,1)S(1)}, bf16[128,128]{0,1:T(8,128)(2,1)S(1)}, bf16[128,128]{0,...) fusion(f32[12,128,128]{1,2,0:T(8,128)S(1)} %get-tuple-element.6, ...), kind=kLoop, calls=%fused_computation.4.clone.1 | loop fusion | flops 9894304 | bytes 2372352 | tf_op jit(solution)/shard_map/while/body/eval_jaxpr/reduce_sum | solution.py:70
  69.9 3.9 %collective-permute-done = f32[128,512]{0,1:T(8,128)S(1)} collective-permute-done((f32[128,512]{0,1:T(8,128)S(1)}, f32[128,512]{0,1:T(8,128)S(1)}, u32[]{:S(2)}, u32[]{:S(2)}) %collective-permute-start) | collective-permute-done | bytes 262176 | tf_op jit(solution)/shard_map/while/body/eval_jaxpr/ppermute | solution.py:17
  74.3 1.0 constant_dynamic-slice_fusion.5
  76.1 2.2 %multiply_reduce_fusion.36 = (bf16[128,128]{0,1:T(8,128)(2,1)S(1)}, bf16[128,128]{0,1:T(8,128)(2,1)S(1)}, bf16[128,128]{0,1:T(8,128)(2,1)S(1)}, bf16[128,128]{0,...) fusion(f32[12,128,128]{1,2,0:T(8,128)S(1)} %get-tuple-element.6, ...), kind=kLoop, calls=%fused_computation.4.clone.1 | loop fusion | flops 9894304 | bytes 2372352 | tf_op jit(solution)/shard_map/while/body/eval_jaxpr/reduce_sum | solution.py:70
  80.1 3.0 %collective-permute-done = f32[128,512]{0,1:T(8,128)S(1)} collective-permute-done((f32[128,512]{0,1:T(8,128)S(1)}, f32[128,512]{0,1:T(8,128)S(1)}, u32[]{:S(2)}, u32[]{:S(2)}) %collective-permute-start) | collective-permute-done | bytes 262176 | tf_op jit(solution)/shard_map/while/body/eval_jaxpr/ppermute | solution.py:17
  83.6 1.0 constant_dynamic-slice_fusion.5
  85.4 2.2 %multiply_reduce_fusion.36 = (bf16[128,128]{0,1:T(8,128)(2,1)S(1)}, bf16[128,128]{0,1:T(8,128)(2,1)S(1)}, bf16[128,128]{0,1:T(8,128)(2,1)S(1)}, bf16[128,128]{0,...) fusion(f32[12,128,128]{1,2,0:T(8,128)S(1)} %get-tuple-element.6, ...), kind=kLoop, calls=%fused_computation.4.clone.1 | loop fusion | flops 9894304 | bytes 2372352 | tf_op jit(solution)/shard_map/while/body/eval_jaxpr/reduce_sum | solution.py:70
  89.3 2.1 %collective-permute-done = f32[128,512]{0,1:T(8,128)S(1)} collective-permute-done((f32[128,512]{0,1:T(8,128)S(1)}, f32[128,512]{0,1:T(8,128)S(1)}, u32[]{:S(2)}, u32[]{:S(2)}) %collective-permute-start) | collective-permute-done | bytes 262176 | tf_op jit(solution)/shard_map/while/body/eval_jaxpr/ppermute | solution.py:17
  92.6 8.2 %collective-permute-done.1 = f32[128,512]{1,0:T(8,128)S(1)} collective-permute-done((f32[128,512]{1,0:T(8,128)S(1)}, f32[128,512]{1,0:T(8,128)S(1)}, u32[]{:S(2)}, u32[]{:S(2)}) %collective-permute-start.1) | collective-permute-done | bytes 262176 | tf_op jit(solution)/shard_map/ppermute | solution.py:17
  101.6 30.0 %all-reduce = (f32[12,8]{0,1:T(8,128)S(1)}, f32[12]{0:T(128)S(1)}) all-reduce(f32[12,8]{0,1:T(8,128)S(1)} %get-tuple-element.351, f32[12]{0:T(128)S(1)} %add_reduce_fusion), channel_id=1, replica_groups=mesh['head'=2,'seq'=4,'dp'=4] {'seq','dp'}, use_global_device_ids=true, to_apply=%region_42.43 | all-reduce | flops 108 | bytes 864 | tf_op jit(solution)/shard_map/psum | solution.py:164
  (143 shorter events, 14.9 us)
Async XLA Ops:
  7.2 30.0 %copy-start.1 = (f32[12,8]{0,1:T(8,128)S(1)}, f32[12,8]{0,1:T(8,128)}, u32[]{:S(2)}) copy-start(f32[12,8]{0,1:T(8,128)} %param.11) | copy-start | bytes 1156
  7.2 48.7 %all-gather.2.cloned.1.call-start = ((), (), s32[]{:S(2)}) async-start(), calls=%async_computation.2 | async-start | bytes 1966080 | tf_op jit(solution)/shard_map/all_gather | solution.py:111
  9.2 123.6 %reduce-scatter.3.cloned.1.call-start = ((), (), s32[]{:S(2)}) async-start(), calls=%async_computation.3 | async-start | bytes 393216 | tf_op jit(solution)/shard_map/reduce_scatter | solution.py:160
  55.8 3.2 %copy-start = (bf16[1,128,1536]{1,2,0:T(8,128)(2,1)S(1)}, bf16[1,128,1536]{1,2,0:T(8,128)(2,1)}, u32[]{:S(2)}) copy-start(bf16[1,128,1536]{1,2,0:T(8,128)(2,1)} %copy.105) | copy-start | bytes 1179652
  63.7 10.1 %collective-permute-start = (f32[128,512]{0,1:T(8,128)S(1)}, f32[128,512]{0,1:T(8,128)S(1)}, u32[]{:S(2)}, u32[]{:S(2)}) collective-permute-start(f32[128,512]{0,1:T(8,128)S(1)} %get-tuple-element.685), channel_id=1, source_target_pairs={{12,0},{0,4},{4,8},{8,12},{13,1},{1,5},{5,9},{9,13},{14,2},{2,6},{... | collective-permute-start | bytes 786440 | tf_op jit(solution)/shard_map/while/body/eval_jaxpr/ppermute | solution.py:17
  73.8 9.2 %collective-permute-start = (f32[128,512]{0,1:T(8,128)S(1)}, f32[128,512]{0,1:T(8,128)S(1)}, u32[]{:S(2)}, u32[]{:S(2)}) collective-permute-start(f32[128,512]{0,1:T(8,128)S(1)} %get-tuple-element.685), channel_id=1, source_target_pairs={{12,0},{0,4},{4,8},{8,12},{13,1},{1,5},{5,9},{9,13},{14,2},{2,6},{... | collective-permute-start | bytes 786440 | tf_op jit(solution)/shard_map/while/body/eval_jaxpr/ppermute | solution.py:17
  83.1 8.3 %collective-permute-start = (f32[128,512]{0,1:T(8,128)S(1)}, f32[128,512]{0,1:T(8,128)S(1)}, u32[]{:S(2)}, u32[]{:S(2)}) collective-permute-start(f32[128,512]{0,1:T(8,128)S(1)} %get-tuple-element.685), channel_id=1, source_target_pairs={{12,0},{0,4},{4,8},{8,12},{13,1},{1,5},{5,9},{9,13},{14,2},{2,6},{... | collective-permute-start | bytes 786440 | tf_op jit(solution)/shard_map/while/body/eval_jaxpr/ppermute | solution.py:17
  92.4 40.4 %reduce-scatter.5.cloned.1.call-start = ((), (), s32[]{:S(2)}) async-start(), calls=%async_computation.4 | async-start | bytes 393216 | tf_op jit(solution)/shard_map/reduce_scatter | solution.py:161
  92.6 8.2 %collective-permute-start.1 = (f32[128,512]{1,0:T(8,128)S(1)}, f32[128,512]{1,0:T(8,128)S(1)}, u32[]{:S(2)}, u32[]{:S(2)}) collective-permute-start(f32[128,512]{1,0:T(8,128)S(1)} %copy.133), channel_id=1, source_target_pairs={{12,0},{0,4},{4,8},{8,12},{13,1},{1,5},{5,9},{9,13},{14,2},{2,6},{... | collective-permute-start | bytes 786440 | tf_op jit(solution)/shard_map/ppermute | solution.py:17
Sparse Core Ops, SparseCore 0:
  9.6 46.2 all-gather.1
  92.5 10.9 reduce-scatter.2
  106.4 11.6 reduce-scatter.4
where the time goes:
time: 140 us; the launch traced here: 139 us
  blocking collectives  53.5 us (38%)
  waiting for transfers between devices  30.6 us (22%)
  other arithmetic  17.4 us (12%)
  local copies, waits for them, and re-layouts  14 us (10%)
  between operations  14 us (10%)
  matrix products  8.72 us (6%)
    psum x1, blocking collectives, body(): mix_total, loss_total = lax.psum((mix_sum, kl_rows), ('seq', 'dp'))  30 us
    all_gather x1, blocking collectives, body(): lax.all_gather(student_key, 'seq', axis=1, tiled=True)  23.6 us
    ppermute x4, waiting for transfers between devices, from_behind(): return lax.ppermute(block, axis, route)  17.2 us
    all_gather x1, waiting for transfers between devices, body(): lax.all_gather(teacher_key, 'seq', axis=1, tiled=True)  13.3 us
    reduce_sum x4, other arithmetic, pair_terms(): mixed_rows.append(jnp.sum(head_mix[:, index, None, None] * excess, axis=0))  8.97 us
    unnamed x15, local copies, waits for them, and re-layouts  5.25 us
    dot_general x5, matrix products, block_maps(): jnp.einsum('rhd,khd->hrk', query_t.reshape(row_count, teacher_heads, HD_T...  5.24 us
    reduce_sum x32, local copies, waits for them, and re-layouts, pair_terms(): mixed_rows.append(jnp.sum(head_mix[:, index, None, None] * excess, axis=0))  3.79 us
  transfers between devices with their start and end apart: 7, of which 5 were waited for; matrix products, arithmetic and copies ran while one was open for 21% of the time, Pallas kernels for 0%

commit v1 on v0

v1 whole, which is shorter than its diff:
```python
import functools
import math

import jax
import jax.numpy as jnp
from jax import lax
from jax.experimental import pallas as pl
from jax.experimental.pallas import tpu as pltpu
from jax.sharding import PartitionSpec as P

HEADS_T = 24
HD_T = 128
HEADS_S = 8
HD_S = 64
LOG2E = math.log2(math.e)
LN2 = math.log(2.0)
LIFT_BLOCK = 32
BACK_BLOCK = 16
VMEM_LIMIT = 40 * 1024 * 1024

F32 = jnp.float32
BF16 = jnp.bfloat16


def dot(lhs, rhs, dims=((1,), (0,))):
    return lax.dot_general(lhs, rhs, (dims, ((), ())), preferred_element_type=F32)


def split(value):
    high = value.astype(BF16)
    low = (value - high.astype(F32)).astype(BF16)
    return high, low


def expand_kernel(mix_ref, mix_tr_ref, lift_hi, lift_lo, back_hi, back_lo):
    def kron(values, size):
        rows, columns = values.shape
        lane = lax.broadcasted_iota(jnp.int32, (rows, columns * size), 1)
        spread = jnp.zeros((rows, columns * size), F32)
        for index in range(columns):
            inside = (lane >= index * size) & (lane < (index + 1) * size)
            spread = jnp.where(inside, values[:, index : index + 1], spread)
        full = (rows, size, columns * size)
        sub = lax.broadcasted_iota(jnp.int32, full, 1)
        within = lax.broadcasted_iota(jnp.int32, full, 2) & (size - 1)
        picked = jnp.where(sub == within, spread[:, None, :], 0.0)
        return picked.reshape(rows * size, columns * size)

    scaled = mix_ref[...] * (HD_S ** (-0.5) * LOG2E)
    lift_hi[...], lift_lo[...] = split(kron(scaled, LIFT_BLOCK))
    back_hi[...], back_lo[...] = split(kron(mix_tr_ref[...], BACK_BLOCK))


def expand_mix(head_mix):
    heads = head_mix.shape[0]
    lift = jax.ShapeDtypeStruct((heads * LIFT_BLOCK, HEADS_S * LIFT_BLOCK), BF16)
    back = jax.ShapeDtypeStruct((HEADS_S * BACK_BLOCK, heads * BACK_BLOCK), BF16)
    return pl.pallas_call(expand_kernel, out_shape=(lift, lift, back, back))(head_mix, head_mix.T)


def stacked(refs, columns):
    parts = [ref[0, :, columns] for ref in refs]
    return parts[0] if len(parts) == 1 else jnp.concatenate(parts, axis=0)


def maps_kernel(row_parts, key_parts, heads, *refs):
    refs = list(refs)
    query_t = [refs.pop(0) for _ in range(row_parts)]
    key_t = [refs.pop(0) for _ in range(key_parts)]
    query_s = [refs.pop(0) for _ in range(row_parts)]
    key_s = [refs.pop(0) for _ in range(key_parts)]
    lift_hi, lift_lo, exp_t, exp_l, stu_hi, stu_lo, top, lse, kl, lifted = refs
    keys = stu_hi.shape[1]
    rows = stu_hi.shape[2]
    for index in range(HEADS_S):
        columns = slice(index * HD_S, (index + 1) * HD_S)
        student = dot(stacked(key_s, columns), stacked(query_s, columns), ((1,), (1,)))
        stu_hi[index], stu_lo[index] = split(student)
    for start in range(0, keys, LIFT_BLOCK):
        block = slice(start, start + LIFT_BLOCK)
        high = stu_hi[:, block, :].reshape(HEADS_S * LIFT_BLOCK, rows)
        low = stu_lo[:, block, :].reshape(HEADS_S * LIFT_BLOCK, rows)
        total = dot(lift_hi[...], high) + (dot(lift_hi[...], low) + dot(lift_lo[...], high))
        lifted[:, block, :] = total.reshape(heads, LIFT_BLOCK, rows)
    for head in range(heads):
        columns = slice(head * HD_T, (head + 1) * HD_T)
        teacher = dot(stacked(key_t, columns), stacked(query_t, columns), ((1,), (1,)))
        teacher = teacher * (HD_T ** (-0.5) * LOG2E)
        top_t = jnp.max(teacher, axis=0, keepdims=True)
        prob_t = jnp.exp2(teacher - top_t)
        exp_t[head] = prob_t
        mixed = lifted[head]
        kl[head : head + 1, :] = jnp.sum(prob_t * (teacher - mixed), axis=0, keepdims=True)
        top_l = jnp.max(mixed, axis=0, keepdims=True)
        prob_l = jnp.exp2(mixed - top_l)
        exp_l[head] = prob_l
        top[0, head : head + 1, :] = top_t
        top[1, head : head + 1, :] = top_l
        lse[0, head : head + 1, :] = top_t + jnp.log2(jnp.sum(prob_t, axis=0, keepdims=True))
        lse[1, head : head + 1, :] = top_l + jnp.log2(jnp.sum(prob_l, axis=0, keepdims=True))


def back_kernel(row_parts, key_parts, heads, head_axis, factor, *refs):
    refs = list(refs)
    query_s = [refs.pop(0) for _ in range(row_parts)]
    key_s = [refs.pop(0) for _ in range(key_parts)]
    lse = [refs.pop(0) for _ in range(row_parts)]
    back_hi, back_lo, exp_t, exp_l, stu_hi, stu_lo, top, kl = refs[:8]
    refs = refs[8:]
    scale_t, scale_l, back, query_h, key_h, mix_acc = refs[-6:]
    sums = refs[0]
    pieces = refs[1:-6]
    shards = len(pieces) // (row_parts + key_parts)
    keys, rows = stu_hi.shape[1:]
    part = rows // row_parts

    lse_all = []
    for which in range(2):
        parts = [ref[which] for ref in lse]
        best = functools.reduce(jnp.maximum, parts)
        total = sum(jnp.exp2(value - best) for value in parts)
        lse_all.append(best + jnp.log2(total))
    scale_t[...] = jnp.exp2(top[0] - lse_all[0])
    scale_l[...] = jnp.exp2(top[1] - lse_all[1])
    own = lax.broadcasted_iota(jnp.int32, (heads, rows), 1) < part
    loss = scale_t[...] * kl[...] + jnp.where(own, lse_all[1] - lse_all[0], 0.0)
    loss = jnp.sum(loss, axis=1, keepdims=True) * LN2

    mix_acc[...] = jnp.zeros_like(mix_acc)
    for start in range(0, keys, LIFT_BLOCK):
        block = slice(start, start + LIFT_BLOCK)
        excess = exp_l[:, block, :] * scale_l[...][:, None, :] - exp_t[:, block, :] * scale_t[...][:, None, :]
        high, low = split(excess)
        s_high = stu_hi[:, block, :].reshape(HEADS_S * LIFT_BLOCK, rows)
        s_low = stu_lo[:, block, :].reshape(HEADS_S * LIFT_BLOCK, rows)
        f_high = high.reshape(heads * LIFT_BLOCK, rows)
        f_low = low.reshape(heads * LIFT_BLOCK, rows)
        over_rows = ((1,), (1,))
        mix_acc[...] += dot(f_high, s_high, over_rows) + (
            dot(f_high, s_low, over_rows) + dot(f_low, s_high, over_rows)
        )
        for inner in range(0, LIFT_BLOCK, BACK_BLOCK):
            b_high = high[:, inner : inner + BACK_BLOCK, :].reshape(heads * BACK_BLOCK, rows)
            b_low = low[:, inner : inner + BACK_BLOCK, :].reshape(heads * BACK_BLOCK, rows)
            total = dot(back_hi[...], b_high) + (dot(back_hi[...], b_low) + dot(back_lo[...], b_high))
            back[:, start + inner : start + inner + BACK_BLOCK, :] = total.astype(BF16).reshape(
                HEADS_S, BACK_BLOCK, rows
            )

    acc = mix_acc[...].reshape(heads, LIFT_BLOCK, HEADS_S * LIFT_BLOCK)
    sub = lax.broadcasted_iota(jnp.int32, acc.shape, 1)
    within = lax.broadcasted_iota(jnp.int32, acc.shape, 2) & (LIFT_BLOCK - 1)
    diagonal = jnp.sum(jnp.where(sub == within, acc, 0.0), axis=1)
    lane = lax.broadcasted_iota(jnp.int32, diagonal.shape, 1)
    slot = lax.broadcasted_iota(jnp.int32, sums.shape, 1)
    packed = jnp.where(slot == HEADS_S, loss, 0.0)
    for index in range(HEADS_S):
        inside = (lane >= index * LIFT_BLOCK) & (lane < (index + 1) * LIFT_BLOCK)
        column = jnp.sum(jnp.where(inside, diagonal, 0.0), axis=1, keepdims=True)
        packed = jnp.where(slot == index, column, packed)
    sums[...] = packed

    for index in range(HEADS_S):
        columns = slice(index * HD_S, (index + 1) * HD_S)
        query_h[index] = stacked(query_s, columns)
        key_h[index] = stacked(key_s, columns)
    place = lax.axis_index(head_axis)
    per = HEADS_S // shards
    for shard in range(shards):
        first = lax.rem(place + shard, shards) * per
        for index in range(per):
            tile = back[first + index]
            columns = slice(index * HD_S, (index + 1) * HD_S)
            on_keys = dot(tile, query_h[first + index]) * factor
            on_rows = dot(tile, key_h[first + index], ((0,), (0,))) * factor
            for spot in range(row_parts):
                ref = pieces[shard * row_parts + spot]
                ref[:, columns] = on_rows[spot * part : (spot + 1) * part]
            size = keys // key_parts
            for spot in range(key_parts):
                ref = pieces[shards * row_parts + shard * key_parts + spot]
                ref[:, columns] = on_keys[spot * size : (spot + 1) * size]


def body(teacher_query, teacher_key, student_query, student_key, head_mix):
    shard_rows = teacher_query.shape[1]
    heads = head_mix.shape[0]
    length = lax.axis_size("seq")
    shards = lax.axis_size("head")
    copies = lax.axis_size("dp")
    row_parts = max(size for size in range(1, math.isqrt(length) + 1) if length % size == 0)
    key_parts = length // row_parts
    rows, keys = row_parts * shard_rows, key_parts * shard_rows

    def along_rows(position, step):
        return position // row_parts * row_parts + (position % row_parts + step) % row_parts

    def along_keys(position, step):
        return (position + step * row_parts) % length

    def fetch(value, target, step):
        return lax.ppermute(value, "seq", [(target(i, step), i) for i in range(length)])

    def deliver(value, target, step, turn):
        pairs = [
            (h * length + i, (h + turn) % shards * length + target(i, step))
            for h in range(shards)
            for i in range(length)
        ]
        return lax.ppermute(value, ("head", "seq"), pairs)

    key_s = [student_key] + [fetch(student_key, along_keys, d) for d in range(1, key_parts)]
    query_s = [student_query] + [fetch(student_query, along_rows, d) for d in range(1, row_parts)]
    key_t = [teacher_key] + [fetch(teacher_key, along_keys, d) for d in range(1, key_parts)]
    query_t = [teacher_query] + [fetch(teacher_query, along_rows, d) for d in range(1, row_parts)]
    lift_hi, lift_lo, back_hi, back_lo = expand_mix(head_mix)

    maps = pltpu.VMEM((heads, keys, rows), F32)
    student = pltpu.VMEM((HEADS_S, keys, rows), BF16)
    stats = pltpu.VMEM((2, heads, rows), F32)
    exp_t, exp_l, stu_hi, stu_lo, top, lse, kl = pl.pallas_call(
        functools.partial(maps_kernel, row_parts, key_parts, heads),
        out_shape=(maps, maps, student, student, stats, stats, pltpu.VMEM((heads, rows), F32)),
        scratch_shapes=[pltpu.VMEM((heads, keys, rows), F32)],
        compiler_params=pltpu.CompilerParams(vmem_limit_bytes=VMEM_LIMIT),
        name="maps",
    )(*query_t, *key_t, *query_s, *key_s, lift_hi, lift_lo)

    lse_parts = [lse]
    for step in range(1, row_parts):
        turned = jnp.roll(lse.reshape(2, heads, row_parts, shard_rows), -step, axis=2)
        lse_parts.append(fetch(turned.reshape(lse.shape), along_rows, row_parts - step))

    weight = shard_rows * length / HEADS_T
    width = HEADS_S * HD_S // shards
    piece = jax.ShapeDtypeStruct((shard_rows, width), F32)
    count = shards * (row_parts + key_parts)
    sums, *pieces = pl.pallas_call(
        functools.partial(back_kernel, row_parts, key_parts, heads, "head", weight * HD_S ** (-0.5)),
        out_shape=(jax.ShapeDtypeStruct((heads, 128), F32),) + (piece,) * count,
        scratch_shapes=[
            pltpu.VMEM((heads, rows), F32),
            pltpu.VMEM((heads, rows), F32),
            pltpu.VMEM((HEADS_S, keys, rows), BF16),
            pltpu.VMEM((HEADS_S, rows, HD_S), BF16),
            pltpu.VMEM((HEADS_S, keys, HD_S), BF16),
            pltpu.VMEM((heads * LIFT_BLOCK, HEADS_S * LIFT_BLOCK), F32),
        ],
        compiler_params=pltpu.CompilerParams(vmem_limit_bytes=VMEM_LIMIT),
        name="back",
    )(*query_s, *key_s, *lse_parts, back_hi, back_lo, exp_t, exp_l, stu_hi, stu_lo, top, kl)

    def collect(parts, target, count):
        total = None
        for turn in range(shards):
            for step in range(count):
                part = parts[turn * count + step]
                if turn or step:
                    part = deliver(part, target, step, turn)
                total = part if total is None else total + part
        return total[None]

    def everyone(value, axis):
        size = lax.axis_size(axis)
        total = value
        for step in range(1, size):
            total = total + lax.ppermute(value, axis, [(i, (i + step) % size) for i in range(size)])
        return total

    grad_key = collect(pieces[shards * row_parts :], along_keys, key_parts)
    grad_query = collect(pieces[: shards * row_parts], along_rows, row_parts)
    total = everyone(everyone(sums, "dp"), "seq")
    samples = copies * teacher_query.shape[0] * shard_rows * length
    grad_mix = total[:, :HEADS_S] * (HD_S ** (-0.5) * weight / samples)
    head_loss = total[:, HEADS_S] / samples
    return (grad_query, grad_key, grad_mix, head_loss)


def solution(mesh):
    return jax.shard_map(
        body,
        mesh=mesh,
        in_specs=(
            P("dp", "seq", "head"),
            P("dp", "seq", "head"),
            P("dp", "seq", None),
            P("dp", "seq", None),
            P("head", None),
        ),
        out_specs=(P("dp", "seq", "head"), P("dp", "seq", "head"), P("head", None), P("head")),
        check_vma=False,
    )
```

time: 140 us -> 92.1 us (0.66)
  blocking collectives: 53.5 us -> 0 us
  starting transfers between devices: 0.36 us -> 20.4 us
  other arithmetic: 17.4 us -> 3.92 us
  between operations: 14 us -> 0.71 us
  local copies, waits for them, and re-layouts: 14 us -> 24.7 us
  Pallas kernels: 0 us -> 8.93 us
  matrix products: 8.72 us -> 0 us
  waiting for transfers between devices: 30.6 us -> 32.8 us
    psum x1 -> x0, blocking collectives: 30 us -> none  [body(): mix_total, loss_total = lax.psum((mix_sum, kl_rows), ('seq', 'dp'))]
    all_gather x1 -> x0, blocking collectives: 23.6 us -> none  [body(): lax.all_gather(student_key, 'seq', axis=1, tiled=True)]
    ppermute x4 -> x17, starting transfers between devices: 0.23 us -> 20.4 us  [the longest x6 8.88 us: deliver(): return lax.ppermute(value, ('head', 'seq'), pairs)]
    unnamed x15 -> x48, local copies, waits for them, and re-layouts: 5.25 us -> 24.6 us
    ppermute x4 -> x17, waiting for transfers between devices: 17.2 us -> 32.8 us  [the longest x5 23.1 us: fetch(): lax.ppermute(value, 'seq', [(target(i, step), i) for i in range(length)])]
    all_gather x1 -> x0, waiting for transfers between devices: 13.3 us -> none  [body(): lax.all_gather(teacher_key, 'seq', axis=1, tiled=True)]
    reduce_sum x7 -> x0, other arithmetic: 12.5 us -> none  [the longest x4 8.97 us: pair_terms(): mixed_rows.append(jnp.sum(head_mix[:, index, None, None] * excess, axis=0))]
    pallas_call x0 -> x3, Pallas kernels: none -> 8.93 us  [the longest x1 3.71 us: body(): pl.pallas_call(functools.partial(back_kernel, row_parts, key_parts, heads...]
  transfers between devices with their start and end apart: 7 -> 17, of which waited for: 5 -> 9; matrix products, arithmetic and copies ran while one was open for 21% -> 5% of each run, Pallas kernels for 0% -> 2%
where the time goes in v1:
time: 92.1 us; the launch traced here: 91.4 us
  waiting for transfers between devices  32.8 us (36%)
  local copies, waits for them, and re-layouts  24.7 us (27%)
  starting transfers between devices  20.4 us (22%)
  Pallas kernels  8.93 us (10%)
  other arithmetic  3.92 us (4%)
    unnamed x48, local copies, waits for them, and re-layouts  24.6 us
    ppermute x5, waiting for transfers between devices, fetch(): lax.ppermute(value, 'seq', [(target(i, step), i) for i in range(length)])  23.1 us
    ppermute x6, starting transfers between devices, deliver(): return lax.ppermute(value, ('head', 'seq'), pairs)  8.88 us
    ppermute x6, waiting for transfers between devices, deliver(): return lax.ppermute(value, ('head', 'seq'), pairs)  6.83 us
    ppermute x5, starting transfers between devices, fetch(): lax.ppermute(value, 'seq', [(target(i, step), i) for i in range(length)])  6.7 us
    ppermute x6, starting transfers between devices, everyone(): lax.ppermute(value, axis, [(i, (i + step) % size) for i in range(size)])  4.83 us
    pallas_call x1, Pallas kernels, body(): pl.pallas_call(functools.partial(back_kernel, row_parts, key_parts, heads...  3.71 us
    pallas_call x1, Pallas kernels, body(): pl.pallas_call(functools.partial(maps_kernel, row_parts, key_parts, heads...  3.55 us
  transfers between devices with their start and end apart: 17, of which 9 were waited for; matrix products, arithmetic and copies ran while one was open for 5% of the time, Pallas kernels for 2%

profile of v1, /device:TPU:0, one launch (start us, length us, event | category | flops | bytes accessed | tf_op | source)
XLA Modules:
  0.0 91.4 jit_solution(11646545873045360076)
XLA Ops:
  0.6 3.1 %collective-permute-start.2 = (bf16[1,128,1536]{2,1,0:T(8,128)(2,1)}, bf16[1,128,1536]{2,1,0:T(8,128)(2,1)S(1)}, u32[]{:S(2)}, u32[]{:S(2)}) collective-permute-start(bf16[1,128,1536]{2,1,0:T(8,128)(2,1)} %refs_0_.2), channel_id=1, source_target_pairs={{4,0},{0,4},{12,8},{8,12},{5,1},{1,5},{13,9},{9,13},{6,2},{2,6},{1... | collective-permute-start | bytes 1179656 | tf_op jit(solution)/shard_map/ppermute | solution.py:202
  3.7 2.6 %collective-permute-start.3 = (bf16[1,128,1536]{2,1,0:T(8,128)(2,1)}, bf16[1,128,1536]{2,1,0:T(8,128)(2,1)S(1)}, u32[]{:S(2)}, u32[]{:S(2)}) collective-permute-start(bf16[1,128,1536]{2,1,0:T(8,128)(2,1)} %refs_2_.2), channel_id=1, source_target_pairs={{8,0},{12,4},{0,8},{4,12},{9,1},{13,5},{1,9},{5,13},{10,2},{14,6},... | collective-permute-start | bytes 1179656 | tf_op jit(solution)/shard_map/ppermute | solution.py:202
  6.8 1.4 %copy.11.mix_ref = f32[12,8]{1,0:T(8,128)} copy(f32[12,8]{0,1:T(8,128)} %param.9) | data formatting | bytes 768 | tf_op args[4]
  8.1 1.7 %shard_map.84 = (bf16[384,256]{1,0:T(8,128)(2,1)}, bf16[384,256]{1,0:T(8,128)(2,1)}, bf16[128,192]{1,0:T(8,128)(2,1)}, bf16[128,192]{1,0:T(8,128)(2,1)}) custom-call(f32[12,8]{1,0:T(8,128)} %copy.11.mix_ref, f32[8,12]{1,0:T(8,128)} %bitcast.5), custom_call_target="tpu_custom_call" | custom-call | tf_op jit(solution)/shard_map/pallas_call | solution.py:58
  9.8 16.4 %collective-permute-done.refs_5_.refs_1_ = bf16[1,128,512]{2,1,0:T(8,128)(2,1)S(1)} collective-permute-done((bf16[1,128,512]{2,1,0:T(8,128)(2,1)}, bf16[1,128,512]{2,1,0:T(8,128)(2,1)S(1)}, u32[]{:S(2)}, u32[]{:S(2)}) %collective-permute-start) | collective-permute-done | bytes 131104 | tf_op jit(solution)/shard_map/ppermute | solution.py:202
  26.2 3.3 %collective-permute-done.1.refs_7_.refs_3_ = bf16[1,128,512]{2,1,0:T(8,128)(2,1)S(1)} collective-permute-done((bf16[1,128,512]{2,1,0:T(8,128)(2,1)}, bf16[1,128,512]{2,1,0:T(8,128)(2,1)S(1)}, u32[]{:S(2)}, u32[]{:S(2)}) %collective-permute-start.1) | collective-permute-done | bytes 131104 | tf_op jit(solution)/shard_map/ppermute | solution.py:202
  38.7 3.5 %maps.1 = (f32[12,256,256]{2,1,0:T(8,128)S(1)}, f32[12,256,256]{2,1,0:T(8,128)S(1)}, bf16[8,256,256]{2,1,0:T(8,128)(2,1)S(1)}, bf16[8,256,256]{2,1,0:T(8,128)(2,...) custom-call(bf16[1,128,1536]{2,1,0:T(8,128)(2,1)S(1)} %copy-done.10, ...), custom_call_target="tpu_custom_call" | custom-call | tf_op jit(solution)/shard_map/maps/pallas_call | solution.py:221
  42.2 1.6 %copy-done = f32[12,256,256]{2,1,0:T(8,128)} copy-done((f32[12,256,256]{2,1,0:T(8,128)}, f32[12,256,256]{2,1,0:T(8,128)S(1)}, u32[]{:S(2)}) %copy-start) | copy-done | bytes 3145752
  46.5 3.4 %collective-permute-done.4.refs_5_ = f32[2,12,256]{2,1,0:T(8,128)S(1)} collective-permute-done((f32[2,12,256]{2,1,0:T(8,128)S(1)}, f32[2,12,256]{2,1,0:T(8,128)S(1)}, u32[]{:S(2)}, u32[]{:S(2)}) %collective-permute-start.4) | collective-permute-done | bytes 24608 | tf_op jit(solution)/shard_map/ppermute | solution.py:202
  50.0 1.9 %copy-done.1 = f32[12,256,256]{2,1,0:T(8,128)S(1)} copy-done((f32[12,256,256]{2,1,0:T(8,128)S(1)}, f32[12,256,256]{2,1,0:T(8,128)}, u32[]{:S(2)}) %copy-start.1) | copy-done | bytes 3145752
  51.8 1.2 %copy-done.3 = bf16[8,256,256]{2,1,0:T(8,128)(2,1)S(1)} copy-done((bf16[8,256,256]{2,1,0:T(8,128)(2,1)S(1)}, bf16[8,256,256]{2,1,0:T(8,128)(2,1)}, u32[]{:S(2)}) %copy-start.3) | copy-done | bytes 1048600
  57.8 3.7 %back.1 = (f32[12,128]{1,0:T(8,128)S(1)}, f32[128,256]{1,0:T(8,128)S(1)}, f32[128,256]{1,0:T(8,128)}, f32[128,256]{1,0:T(8,128)}, f32[128,256]{1,0:T(8,128)}, /*...) custom-call(bf16[1,128,512]{2,1,0:T(8,128)(2,1)S(1)} %copy-done.7, ...), custom_call_target="tpu_custom_call" | custom-call | tf_op jit(solution)/shard_map/back/pallas_call | solution.py:238
  63.4 1.5 %collective-permute-start.12 = (f32[12,128]{1,0:T(8,128)S(1)}, f32[12,128]{1,0:T(8,128)S(1)}, u32[]{:S(2)}, u32[]{:S(2)}) collective-permute-start(f32[12,128]{1,0:T(8,128)S(1)} %get-tuple-element.43), channel_id=1, source_target_pairs={{0,2},{1,3},{2,0},{3,1},{4,6},{5,7},{6,4},{7,5},{8,10},{9,11},{10,... | collective-permute-start | bytes 18440 | tf_op jit(solution)/shard_map/ppermute | solution.py:267
  65.2 1.9 %collective-permute-done.12 = f32[12,128]{1,0:T(8,128)S(1)} collective-permute-done((f32[12,128]{1,0:T(8,128)S(1)}, f32[12,128]{1,0:T(8,128)S(1)}, u32[]{:S(2)}, u32[]{:S(2)}) %collective-permute-start.12) | collective-permute-done | bytes 6176 | tf_op jit(solution)/shard_map/ppermute | solution.py:267
  68.0 2.5 %collective-permute-start.16 = (f32[12,128]{1,0:T(8,128)S(1)}, f32[12,128]{1,0:T(8,128)S(1)}, u32[]{:S(2)}, u32[]{:S(2)}) collective-permute-start(f32[12,128]{1,0:T(8,128)S(1)} %add_add_fusion.1), channel_id=1, source_target_pairs={{0,12},{4,0},{8,4},{12,8},{1,13},{5,1},{9,5},{13,9},{2,14},{6,2},{... | collective-permute-start | bytes 18440 | tf_op jit(solution)/shard_map/ppermute | solution.py:267
  71.1 2.9 %collective-permute-start.5 = (f32[128,256]{1,0:T(8,128)}, f32[128,256]{1,0:T(8,128)S(1)}, u32[]{:S(2)}, u32[]{:S(2)}) collective-permute-start(f32[128,256]{1,0:T(8,128)} %get-tuple-element.36), channel_id=1, source_target_pairs={{0,4},{4,0},{8,12},{12,8},{16,20},{20,16},{24,28},{28,24},{1,5},{5... | collective-permute-start | bytes 393224 | tf_op jit(solution)/shard_map/ppermute | solution.py:210
  74.0 1.6 %collective-permute-start.6 = (f32[128,256]{1,0:T(8,128)}, f32[128,256]{1,0:T(8,128)S(1)}, u32[]{:S(2)}, u32[]{:S(2)}) collective-permute-start(f32[128,256]{1,0:T(8,128)} %get-tuple-element.37), channel_id=1, source_target_pairs={{0,16},{4,20},{8,24},{12,28},{16,0},{20,4},{24,8},{28,12},{1,17},{... | collective-permute-start | bytes 393224 | tf_op jit(solution)/shard_map/ppermute | solution.py:210
  75.6 2.1 %collective-permute-start.8 = (f32[128,256]{1,0:T(8,128)}, f32[128,256]{1,0:T(8,128)S(1)}, u32[]{:S(2)}, u32[]{:S(2)}) collective-permute-start(f32[128,256]{1,0:T(8,128)} %get-tuple-element.40), channel_id=1, source_target_pairs={{0,8},{4,12},{8,0},{12,4},{16,24},{20,28},{24,16},{28,20},{1,9},{5... | collective-permute-start | bytes 393224 | tf_op jit(solution)/shard_map/ppermute | solution.py:210
  79.9 1.5 %collective-permute-start.10 = (f32[128,256]{1,0:T(8,128)}, f32[128,256]{1,0:T(8,128)S(1)}, u32[]{:S(2)}, u32[]{:S(2)}) collective-permute-start(f32[128,256]{1,0:T(8,128)} %copy-done.22), channel_id=1, source_target_pairs={{0,24},{4,28},{8,16},{12,20},{16,8},{20,12},{24,0},{28,4},{1,25},{... | collective-permute-start | bytes 393224 | tf_op jit(solution)/shard_map/ppermute | solution.py:210
  81.9 1.4 %collective-permute-done.7 = f32[128,256]{1,0:T(8,128)S(1)} collective-permute-done((f32[128,256]{1,0:T(8,128)}, f32[128,256]{1,0:T(8,128)S(1)}, u32[]{:S(2)}, u32[]{:S(2)}) %collective-permute-start.7) | collective-permute-done | bytes 131104 | tf_op jit(solution)/shard_map/ppermute | solution.py:210
  83.4 1.6 %add_bitcast_fusion.1 = f32[1,128,256]{2,1,0:T(8,128)} fusion(f32[128,256]{1,0:T(8,128)S(1)} %collective-permute-done.7, f32[128,256]{1,0:T(8,128)S(1)} %collective-permute-done.6, f32[128,256]{1,0:T(8,128)} %copy-done.19, f32[128,256]{1,0:T(8,128)S(1)} %collective-permute-done.5), kind=kLoop, calls=%fused_computation.1 | loop fusion | flops 98304 | bytes 655360 | tf_op jit(solution)/shard_map/broadcast_in_dim | solution.py:261
  85.0 2.4 %collective-permute-done.8 = f32[128,256]{1,0:T(8,128)S(1)} collective-permute-done((f32[128,256]{1,0:T(8,128)}, f32[128,256]{1,0:T(8,128)S(1)}, u32[]{:S(2)}, u32[]{:S(2)}) %collective-permute-start.8) | collective-permute-done | bytes 131104 | tf_op jit(solution)/shard_map/ppermute | solution.py:210
  87.4 2.4 %collective-permute-done.10 = f32[128,256]{1,0:T(8,128)S(1)} collective-permute-done((f32[128,256]{1,0:T(8,128)}, f32[128,256]{1,0:T(8,128)S(1)}, u32[]{:S(2)}, u32[]{:S(2)}) %collective-permute-start.10) | collective-permute-done | bytes 131104 | tf_op jit(solution)/shard_map/ppermute | solution.py:210
  89.8 1.6 %add_bitcast_fusion = f32[1,128,256]{2,1,0:T(8,128)} fusion(f32[128,256]{1,0:T(8,128)S(1)} %collective-permute-done.10, f32[128,256]{1,0:T(8,128)S(1)} %collective-permute-done.9, f32[128,256]{1,0:T(8,128)} %copy-done.18, f32[128,256]{1,0:T(8,128)S(1)} %collective-permute-done.8), kind=kLoop, calls=%fused_computation | loop fusion | flops 98304 | bytes 655360 | tf_op jit(solution)/shard_map/broadcast_in_dim | solution.py:261
  (71 shorter events, 23.5 us)
Async XLA Ops:
  0.6 28.9 %collective-permute-start.2 = (bf16[1,128,1536]{2,1,0:T(8,128)(2,1)}, bf16[1,128,1536]{2,1,0:T(8,128)(2,1)S(1)}, u32[]{:S(2)}, u32[]{:S(2)}) collective-permute-start(bf16[1,128,1536]{2,1,0:T(8,128)(2,1)} %refs_0_.2), channel_id=1, source_target_pairs={{4,0},{0,4},{12,8},{8,12},{5,1},{1,5},{13,9},{9,13},{6,2},{2,6},{1... | collective-permute-start | bytes 1179656 | tf_op jit(solution)/shard_map/ppermute | solution.py:202
  3.7 26.5 %collective-permute-start.3 = (bf16[1,128,1536]{2,1,0:T(8,128)(2,1)}, bf16[1,128,1536]{2,1,0:T(8,128)(2,1)S(1)}, u32[]{:S(2)}, u32[]{:S(2)}) collective-permute-start(bf16[1,128,1536]{2,1,0:T(8,128)(2,1)} %refs_2_.2), channel_id=1, source_target_pairs={{8,0},{12,4},{0,8},{4,12},{9,1},{13,5},{1,9},{5,13},{10,2},{14,6},... | collective-permute-start | bytes 1179656 | tf_op jit(solution)/shard_map/ppermute | solution.py:202
  6.3 19.9 %collective-permute-start = (bf16[1,128,512]{2,1,0:T(8,128)(2,1)}, bf16[1,128,512]{2,1,0:T(8,128)(2,1)S(1)}, u32[]{:S(2)}, u32[]{:S(2)}) collective-permute-start(bf16[1,128,512]{2,1,0:T(8,128)(2,1)} %refs_0_.3), channel_id=1, source_target_pairs={{4,0},{0,4},{12,8},{8,12},{5,1},{1,5},{13,9},{9,13},{6,2},{2,6},{1... | collective-permute-start | bytes 393224 | tf_op jit(solution)/shard_map/ppermute | solution.py:202
  6.8 22.7 %collective-permute-start.1 = (bf16[1,128,512]{2,1,0:T(8,128)(2,1)}, bf16[1,128,512]{2,1,0:T(8,128)(2,1)S(1)}, u32[]{:S(2)}, u32[]{:S(2)}) collective-permute-start(bf16[1,128,512]{2,1,0:T(8,128)(2,1)} %refs_2_.3), channel_id=1, source_target_pairs={{8,0},{12,4},{0,8},{4,12},{9,1},{13,5},{1,9},{5,13},{10,2},{14,6},... | collective-permute-start | bytes 393224 | tf_op jit(solution)/shard_map/ppermute | solution.py:202
  32.8 1.0 %copy-start.10 = (bf16[1,128,1536]{2,1,0:T(8,128)(2,1)S(1)}, bf16[1,128,1536]{2,1,0:T(8,128)(2,1)}, u32[]{:S(2)}) copy-start(bf16[1,128,1536]{2,1,0:T(8,128)(2,1)} %refs_0_.2) | copy-start | bytes 1179652
  42.2 1.6 %copy-start = (f32[12,256,256]{2,1,0:T(8,128)}, f32[12,256,256]{2,1,0:T(8,128)S(1)}, u32[]{:S(2)}) copy-start(f32[12,256,256]{2,1,0:T(8,128)S(1)} %get-tuple-element.30.refs_9_) | copy-start | bytes 9437188
  43.8 1.0 %copy-start.2 = (bf16[8,256,256]{2,1,0:T(8,128)(2,1)}, bf16[8,256,256]{2,1,0:T(8,128)(2,1)S(1)}, u32[]{:S(2)}) copy-start(bf16[8,256,256]{2,1,0:T(8,128)(2,1)S(1)} %get-tuple-element.31.refs_10_) | copy-start | bytes 3145732
  44.8 1.0 %copy-start.4 = (bf16[8,256,256]{2,1,0:T(8,128)(2,1)}, bf16[8,256,256]{2,1,0:T(8,128)(2,1)S(1)}, u32[]{:S(2)}) copy-start(bf16[8,256,256]{2,1,0:T(8,128)(2,1)S(1)} %get-tuple-element.32.refs_11_) | copy-start | bytes 3145732
  46.0 4.0 %collective-permute-start.4 = (f32[2,12,256]{2,1,0:T(8,128)S(1)}, f32[2,12,256]{2,1,0:T(8,128)S(1)}, u32[]{:S(2)}, u32[]{:S(2)}) collective-permute-start(f32[2,12,256]{2,1,0:T(8,128)S(1)} %reshape.19), channel_id=1, source_target_pairs={{4,0},{0,4},{12,8},{8,12},{5,1},{1,5},{13,9},{9,13},{6,2},{2,6},{1... | collective-permute-start | bytes 73736 | tf_op jit(solution)/shard_map/ppermute | solution.py:202
  49.9 1.9 %copy-start.1 = (f32[12,256,256]{2,1,0:T(8,128)S(1)}, f32[12,256,256]{2,1,0:T(8,128)}, u32[]{:S(2)}) copy-start(f32[12,256,256]{2,1,0:T(8,128)} %copy-done) | copy-start | bytes 9437188
  51.8 1.2 %copy-start.3 = (bf16[8,256,256]{2,1,0:T(8,128)(2,1)S(1)}, bf16[8,256,256]{2,1,0:T(8,128)(2,1)}, u32[]{:S(2)}) copy-start(bf16[8,256,256]{2,1,0:T(8,128)(2,1)} %copy-done.2) | copy-start | bytes 3145732
  53.1 1.2 %copy-start.5 = (bf16[8,256,256]{2,1,0:T(8,128)(2,1)S(1)}, bf16[8,256,256]{2,1,0:T(8,128)(2,1)}, u32[]{:S(2)}) copy-start(bf16[8,256,256]{2,1,0:T(8,128)(2,1)} %copy-done.4) | copy-start | bytes 3145732
  63.4 1.7 %collective-permute-start.13 = (f32[12,128]{1,0:T(8,128)S(1)}, f32[12,128]{1,0:T(8,128)S(1)}, u32[]{:S(2)}, u32[]{:S(2)}) collective-permute-start(f32[12,128]{1,0:T(8,128)S(1)} %get-tuple-element.43), channel_id=1, source_target_pairs={{0,3},{1,0},{2,1},{3,2},{4,7},{5,4},{6,5},{7,6},{8,11},{9,8},{10,9... | collective-permute-start | bytes 18440 | tf_op jit(solution)/shard_map/ppermute | solution.py:267
  63.4 3.7 %collective-permute-start.12 = (f32[12,128]{1,0:T(8,128)S(1)}, f32[12,128]{1,0:T(8,128)S(1)}, u32[]{:S(2)}, u32[]{:S(2)}) collective-permute-start(f32[12,128]{1,0:T(8,128)S(1)} %get-tuple-element.43), channel_id=1, source_target_pairs={{0,2},{1,3},{2,0},{3,1},{4,6},{5,7},{6,4},{7,5},{8,10},{9,11},{10,... | collective-permute-start | bytes 18440 | tf_op jit(solution)/shard_map/ppermute | solution.py:267
  64.9 3.1 %collective-permute-start.11 = (f32[12,128]{1,0:T(8,128)S(1)}, f32[12,128]{1,0:T(8,128)S(1)}, u32[]{:S(2)}, u32[]{:S(2)}) collective-permute-start(f32[12,128]{1,0:T(8,128)S(1)} %get-tuple-element.43), channel_id=1, source_target_pairs={{0,1},{1,2},{2,3},{3,0},{4,5},{5,6},{6,7},{7,4},{8,9},{9,10},{10,1... | collective-permute-start | bytes 18440 | tf_op jit(solution)/shard_map/ppermute | solution.py:267
  68.0 7.5 %collective-permute-start.16 = (f32[12,128]{1,0:T(8,128)S(1)}, f32[12,128]{1,0:T(8,128)S(1)}, u32[]{:S(2)}, u32[]{:S(2)}) collective-permute-start(f32[12,128]{1,0:T(8,128)S(1)} %add_add_fusion.1), channel_id=1, source_target_pairs={{0,12},{4,0},{8,4},{12,8},{1,13},{5,1},{9,5},{13,9},{2,14},{6,2},{... | collective-permute-start | bytes 18440 | tf_op jit(solution)/shard_map/ppermute | solution.py:267
  70.5 5.1 %collective-permute-start.15 = (f32[12,128]{1,0:T(8,128)S(1)}, f32[12,128]{1,0:T(8,128)S(1)}, u32[]{:S(2)}, u32[]{:S(2)}) collective-permute-start(f32[12,128]{1,0:T(8,128)S(1)} %add_add_fusion.1), channel_id=1, source_target_pairs={{0,8},{4,12},{8,0},{12,4},{1,9},{5,13},{9,1},{13,5},{2,10},{6,14},... | collective-permute-start | bytes 18440 | tf_op jit(solution)/shard_map/ppermute | solution.py:267
  70.5 7.1 %collective-permute-start.14 = (f32[12,128]{1,0:T(8,128)S(1)}, f32[12,128]{1,0:T(8,128)S(1)}, u32[]{:S(2)}, u32[]{:S(2)}) collective-permute-start(f32[12,128]{1,0:T(8,128)S(1)} %add_add_fusion.1), channel_id=1, source_target_pairs={{0,4},{4,8},{8,12},{12,0},{1,5},{5,9},{9,13},{13,1},{2,6},{6,10},{... | collective-permute-start | bytes 18440 | tf_op jit(solution)/shard_map/ppermute | solution.py:267
  71.1 8.7 %collective-permute-start.5 = (f32[128,256]{1,0:T(8,128)}, f32[128,256]{1,0:T(8,128)S(1)}, u32[]{:S(2)}, u32[]{:S(2)}) collective-permute-start(f32[128,256]{1,0:T(8,128)} %get-tuple-element.36), channel_id=1, source_target_pairs={{0,4},{4,0},{8,12},{12,8},{16,20},{20,16},{24,28},{28,24},{1,5},{5... | collective-permute-start | bytes 393224 | tf_op jit(solution)/shard_map/ppermute | solution.py:210
  74.0 8.0 %collective-permute-start.6 = (f32[128,256]{1,0:T(8,128)}, f32[128,256]{1,0:T(8,128)S(1)}, u32[]{:S(2)}, u32[]{:S(2)}) collective-permute-start(f32[128,256]{1,0:T(8,128)} %get-tuple-element.37), channel_id=1, source_target_pairs={{0,16},{4,20},{8,24},{12,28},{16,0},{20,4},{24,8},{28,12},{1,17},{... | collective-permute-start | bytes 393224 | tf_op jit(solution)/shard_map/ppermute | solution.py:210
  75.6 7.8 %collective-permute-start.7 = (f32[128,256]{1,0:T(8,128)}, f32[128,256]{1,0:T(8,128)S(1)}, u32[]{:S(2)}, u32[]{:S(2)}) collective-permute-start(f32[128,256]{1,0:T(8,128)} %get-tuple-element.38), channel_id=1, source_target_pairs={{0,20},{4,16},{8,28},{12,24},{16,4},{20,0},{24,12},{28,8},{1,21},{... | collective-permute-start | bytes 393224 | tf_op jit(solution)/shard_map/ppermute | solution.py:210
  75.6 11.8 %collective-permute-start.8 = (f32[128,256]{1,0:T(8,128)}, f32[128,256]{1,0:T(8,128)S(1)}, u32[]{:S(2)}, u32[]{:S(2)}) collective-permute-start(f32[128,256]{1,0:T(8,128)} %get-tuple-element.40), channel_id=1, source_target_pairs={{0,8},{4,12},{8,0},{12,4},{16,24},{20,28},{24,16},{28,20},{1,9},{5... | collective-permute-start | bytes 393224 | tf_op jit(solution)/shard_map/ppermute | solution.py:210
  77.6 9.8 %collective-permute-start.9 = (f32[128,256]{1,0:T(8,128)}, f32[128,256]{1,0:T(8,128)S(1)}, u32[]{:S(2)}, u32[]{:S(2)}) collective-permute-start(f32[128,256]{1,0:T(8,128)} %get-tuple-element.41), channel_id=1, source_target_pairs={{0,16},{4,20},{8,24},{12,28},{16,0},{20,4},{24,8},{28,12},{1,17},{... | collective-permute-start | bytes 393224 | tf_op jit(solution)/shard_map/ppermute | solution.py:210
  79.9 10.0 %collective-permute-start.10 = (f32[128,256]{1,0:T(8,128)}, f32[128,256]{1,0:T(8,128)S(1)}, u32[]{:S(2)}, u32[]{:S(2)}) collective-permute-start(f32[128,256]{1,0:T(8,128)} %copy-done.22), channel_id=1, source_target_pairs={{0,24},{4,28},{8,16},{12,20},{16,8},{20,12},{24,0},{28,4},{1,25},{... | collective-permute-start | bytes 393224 | tf_op jit(solution)/shard_map/ppermute | solution.py:210
  (16 other events, 13.6 us)
